TPU v7x, 256 devices: a whole 4x4x8 slice. The times are simulated.
256 devices in a mesh: sec: 16 (over z, core), op: 16 (over x, y).
Axes of the slice: x: 4, y: 4, z: 8, core: 2. Of those that a mesh axis runs over, the one named last changes fastest.
Arguments:
- theta: float32 [32, 512, 512], P('sec', 'op'), may hold values from -6 to 6
- counts: int32 [32], P('sec'), may hold values from 256 to 512, as said below
- pair_source: int32 [256], P('sec'), may hold values from 0 to 1
- pair_target: int32 [256], P('sec'), may hold values from 0 to 31
- left_ops: float32 [1024, 512, 512], P(('sec', 'op')), may hold values from -0.25 to 0.25
- right_ops: float32 [1024, 512, 512], P(('sec', 'op')), may hold values from -0.25 to 0.25
Outputs:
- cheb_last: float32 [32, 512, 512], P('sec', 'op')
- cheb_prev: float32 [32, 512, 512], P('sec', 'op')
Inputs may be any that keep to these rules, and one draw needn't show every extreme that they name: `counts`: every sector has between 256 and 512 live states; some sector has exactly 512 and some exactly 256.
All inputs are finite; a program needn't handle non-finite values.
Results may differ from a plain program's by a relative error of at most 0.0001.
Values sent between devices are 32-bit elements; how exact they have to be, the bound alone decides.
A program may use at most 64 MiB of HBM per device.

v0:
```python
import math
import jax
import jax.numpy as jnp
from jax import lax
from jax.sharding import PartitionSpec as P

STEPS = 3


def per_device(theta, counts, pair_source, pair_target, left_ops, right_ops):
    op_count = lax.axis_size("op")
    op_place = lax.axis_index("op")
    sec_place = lax.axis_index("sec")
    sec_local = theta.shape[0]
    row_count = theta.shape[1]
    order_size = theta.shape[2]
    pairs_local = left_ops.shape[0]
    group_blocks = pair_target.shape[0]
    sectors_all = sec_local * lax.axis_size("sec")
    factor = 0.5 / math.sqrt(group_blocks * pairs_local / sec_local)
    highest = lax.Precision.HIGHEST
    my_source = lax.dynamic_index_in_dim(pair_source, op_place, 0, keepdims=False)
    row_numbers = op_place * row_count + jnp.arange(row_count, dtype=jnp.int32)
    row_alive = row_numbers[None, :] < counts[:, None]
    column_alive = jnp.arange(order_size, dtype=jnp.int32)[None, :] < counts[:, None]
    live_mask = (row_alive[:, :, None] & column_alive[:, None, :]).astype(jnp.float32)
    target_hot = (pair_target[None, :] == jnp.arange(sectors_all, dtype=jnp.int32)[:, None]).astype(
        jnp.float32
    )

    def hamiltonian(iterate):
        gathered = lax.all_gather(iterate, "op", axis=1, tiled=True)
        chosen = lax.dynamic_index_in_dim(gathered, my_source, 0, keepdims=False)
        left_product = jnp.einsum("pmr,rn->pmn", left_ops, chosen, precision=highest)
        block_term = jnp.einsum("pmk,pnk->mn", left_product, right_ops, precision=highest)
        split_rows = block_term.reshape(op_count, row_count, order_size)
        block_rows = lax.all_to_all(split_rows, "op", split_axis=0, concat_axis=0, tiled=True)
        flat_rows = block_rows.reshape(group_blocks, row_count * order_size)
        sector_sums = jnp.dot(
            target_hot, flat_rows, precision=highest, preferred_element_type=jnp.float32
        )
        sector_sums = sector_sums.reshape(sectors_all, row_count, order_size)
        whole_sums = lax.psum(sector_sums, "sec")
        own_sums = lax.dynamic_slice_in_dim(whole_sums, sec_place * sec_local, sec_local, 0)
        return factor * own_sums * live_mask

    previous = theta * live_mask
    current = hamiltonian(previous)
    for step_number in range(STEPS - 1):
        following = 2.0 * hamiltonian(current) - previous
        previous, current = (current, following)
    return (current, previous)


def solution(mesh):
    in_specs = (
        P("sec", "op", None),
        P("sec"),
        P("sec"),
        P("sec"),
        P(("sec", "op"), None, None),
        P(("sec", "op"), None, None),
    )
    out_specs = (P("sec", "op", None), P("sec", "op", None))
    return jax.shard_map(
        per_device, mesh=mesh, in_specs=in_specs, out_specs=out_specs, check_vma=False
    )
```

profile of v0, /device:TPU:1, one launch (start us, length us, event | category | flops | bytes accessed | tf_op | source)
XLA Modules:
  0.0 675.0 jit_solution(8471230393268469698)
XLA Ops:
  7.2 0.0 all-gather.4.cloned.1.call-start
  7.2 0.7 iota_compare_fusion.1
  8.0 0.7 broadcast_compare_fusion
  8.7 1.7 and_select_fusion.3
  10.4 0.0 all-gather.4.cloned.1.call-update
  10.4 0.0 all-reduce.4.cloned.1.call-start
  10.5 1.2 dynamic_slice.23
  13.7 50.3 %all-gather.4.cloned.1.call-done = f32[2,512,512]{2,0,1:T(2,128)} async-done(((f32[2,32,512]{2,0,1:T(2,128)}), f32[2,512,512]{2,0,1:T(2,128)}) %all-gather.4.cloned.1.call-update) | async-done | bytes 2097168 | tf_op jit(solution)/shard_map/all_gather | solution.py:32
  63.9 2.5 constant_dynamic-slice_fusion.2
  66.4 1.3 copy.18
  67.8 0.0 copy-start
  67.8 10.3 %fusion.19 = f32[512,4,512]{2,0,1:T(8,128)S(1)} fusion(f32[4,512,512]{2,1,0:T(8,128)} %param.10, f32[1,512,512]{1,2,0:T(8,128)S(1)} %copy.18), kind=kOutput, calls=%fused_computation.19 | convolution fusion | flops 6442450944 | bytes 9437184 | tf_op jit(solution)/shard_map/pmr,rn->pmn/dot_general | solution.py:34
  78.1 13.9 %fusion.4 = f32[512,512,1]{1,0,2:T(8,128)S(1)} fusion(f32[4,512,512]{2,1,0:T(8,128)S(1)} %copy-done, f32[512,4,512]{2,0,1:T(8,128)S(1)} %fusion.19), kind=kOutput, calls=%fused_computation.4 | convolution fusion | flops 6442450944 | bytes 9437184 | tf_op jit(solution)/shard_map/pmk,pnk->mn/dot_general | solution.py:35
  92.0 19.3 %all_to_all.15 = f32[16,32,512]{2,1,0:T(8,128)S(1)} all-to-all(f32[16,32,512]{2,1,0:T(8,128)S(1)} %bitcast.75), channel_id=1, replica_groups=mesh['sec'=16,'op'=16] {'op'}, dimensions={0} | all-to-all | bytes 2097152 | tf_op jit(solution)/shard_map/all_to_all | solution.py:37
  111.3 2.9 fusion.12
  114.2 0.0 all-reduce.4.cloned.1.call-update
  114.2 0.0 all-gather.6.cloned.1.call-start
  114.2 115.1 %all-reduce.4.cloned.1.call-done = f32[32,32,512]{2,0,1:T(8,128)} async-done(((f32[32,32,512]{2,0,1:T(8,128)}), f32[32,32,512]{2,0,1:T(8,128)}) %all-reduce.4.cloned.1.call-update) | async-done | bytes 2097168 | tf_op jit(solution)/shard_map/psum | solution.py:43
  229.4 1.8 and_select_fusion.2
  231.2 0.0 all-gather.6.cloned.1.call-update
  231.3 0.0 all-reduce.6.cloned.1.call-start
  231.3 50.7 %all-gather.6.cloned.1.call-done = f32[2,512,512]{2,0,1:T(2,128)} async-done(((f32[2,32,512]{2,0,1:T(2,128)}), f32[2,512,512]{2,0,1:T(2,128)}) %all-gather.6.cloned.1.call-update) | async-done | bytes 2097168 | tf_op jit(solution)/shard_map/all_gather | solution.py:32
  282.0 2.5 constant_dynamic-slice_fusion.1
  284.5 1.3 copy.21
  285.8 10.3 %fusion.17 = f32[512,4,512]{2,0,1:T(8,128)S(1)} fusion(f32[4,512,512]{2,1,0:T(8,128)} %param.10, f32[1,512,512]{1,2,0:T(8,128)S(1)} %copy.21), kind=kOutput, calls=%fused_computation.17 | convolution fusion | flops 6442450944 | bytes 9437184 | tf_op jit(solution)/shard_map/pmr,rn->pmn/dot_general | solution.py:34
  296.1 13.7 %fusion.2 = f32[512,512,1]{1,0,2:T(8,128)S(1)} fusion(f32[4,512,512]{2,1,0:T(8,128)S(1)} %copy-done.1, f32[512,4,512]{2,0,1:T(8,128)S(1)} %fusion.17), kind=kOutput, calls=%fused_computation.2 | convolution fusion | flops 6442450944 | bytes 9437184 | tf_op jit(solution)/shard_map/pmk,pnk->mn/dot_general | solution.py:35
  309.8 0.0 copy-start.4
  309.9 19.4 %all_to_all.16 = f32[16,32,512]{2,1,0:T(8,128)S(1)} all-to-all(f32[16,32,512]{2,1,0:T(8,128)S(1)} %bitcast.76), channel_id=1, replica_groups=mesh['sec'=16,'op'=16] {'op'}, dimensions={0} | all-to-all | bytes 2097152 | tf_op jit(solution)/shard_map/all_to_all | solution.py:37
  329.2 2.9 fusion.9
  332.1 0.0 all-reduce.6.cloned.1.call-update
  332.2 0.0 all-gather.8.cloned.1.call-start
  332.2 115.3 %all-reduce.6.cloned.1.call-done = f32[32,32,512]{2,0,1:T(8,128)} async-done(((f32[32,32,512]{2,0,1:T(8,128)}), f32[32,32,512]{2,0,1:T(8,128)}) %all-reduce.6.cloned.1.call-update) | async-done | bytes 2097168 | tf_op jit(solution)/shard_map/psum | solution.py:43
  447.5 1.9 fusion.22
  449.5 0.0 all-gather.8.cloned.1.call-update
  449.5 0.0 all-reduce.8.cloned.1.call-start
  449.5 50.4 %all-gather.8.cloned.1.call-done = f32[2,512,512]{2,0,1:T(2,128)} async-done(((f32[2,32,512]{2,0,1:T(2,128)}), f32[2,512,512]{2,0,1:T(2,128)}) %all-gather.8.cloned.1.call-update) | async-done | bytes 2097168 | tf_op jit(solution)/shard_map/all_gather | solution.py:32
  500.0 2.5 constant_dynamic-slice_fusion
  502.5 1.3 copy.24
  503.8 0.0 copy-start.2
  503.8 10.3 %fusion.15 = f32[512,4,512]{2,0,1:T(8,128)S(1)} fusion(f32[4,512,512]{2,1,0:T(8,128)} %param.10, f32[1,512,512]{1,2,0:T(8,128)S(1)} %copy.24), kind=kOutput, calls=%fused_computation.15 | convolution fusion | flops 6442450944 | bytes 9437184 | tf_op jit(solution)/shard_map/pmr,rn->pmn/dot_general | solution.py:34
  514.1 13.8 %fusion = f32[512,512,1]{1,0,2:T(8,128)S(1)} fusion(f32[4,512,512]{2,1,0:T(8,128)S(1)} %copy-done.2, f32[512,4,512]{2,0,1:T(8,128)S(1)} %fusion.15), kind=kOutput, calls=%fused_computation | convolution fusion | flops 6442450944 | bytes 9437184 | tf_op jit(solution)/shard_map/pmk,pnk->mn/dot_general | solution.py:35
  528.0 19.4 %all_to_all.17 = f32[16,32,512]{2,1,0:T(8,128)S(1)} all-to-all(f32[16,32,512]{2,1,0:T(8,128)S(1)} %bitcast.77), channel_id=1, replica_groups=mesh['sec'=16,'op'=16] {'op'}, dimensions={0} | all-to-all | bytes 2097152 | tf_op jit(solution)/shard_map/all_to_all | solution.py:37
  547.4 2.9 fusion.6
  550.3 0.0 all-reduce.8.cloned.1.call-update
  550.3 0.7 copy.28
  551.0 114.5 %all-reduce.8.cloned.1.call-done = f32[32,32,512]{2,0,1:T(8,128)} async-done(((f32[32,32,512]{2,0,1:T(8,128)}), f32[32,32,512]{2,0,1:T(8,128)}) %all-reduce.8.cloned.1.call-update) | async-done | bytes 2097168 | tf_op jit(solution)/shard_map/psum | solution.py:43
  665.5 1.4 fusion.24
  666.9 0.7 copy.27
  (10 shorter events, 0.0 us)
Async XLA Ops:
  7.2 56.8 %all-gather.4.cloned.1.call-start = ((), (), s32[]{:S(2)}) async-start(), calls=%async_computation.3 | async-start | bytes 2228224 | tf_op jit(solution)/shard_map/all_gather | solution.py:32
  10.4 219.0 %all-reduce.4.cloned.1.call-start = ((), (), s32[]{:S(2)}) async-start(), calls=%async_computation.4 | async-start | bytes 4194304 | tf_op jit(solution)/shard_map/psum | solution.py:43
  67.8 10.3 %copy-start = (f32[4,512,512]{2,1,0:T(8,128)S(1)}, f32[4,512,512]{2,1,0:T(8,128)}, u32[]{:S(2)}) copy-start(f32[4,512,512]{2,1,0:T(8,128)} %param.11) | copy-start | bytes 12582916
  78.1 33.2 %copy-start.5 = (s32[16]{0:T(128)S(1)}, s32[16]{0:T(128)}, u32[]{:S(2)}) copy-start(s32[16]{0:T(128)} %param.9) | copy-start | bytes 196
  114.2 167.8 %all-gather.6.cloned.1.call-start = ((), (), s32[]{:S(2)}) async-start(), calls=%async_computation.5 | async-start | bytes 2228224 | tf_op jit(solution)/shard_map/all_gather | solution.py:32
  231.3 216.3 %all-reduce.6.cloned.1.call-start = ((), (), s32[]{:S(2)}) async-start(), calls=%async_computation.6 | async-start | bytes 4194304 | tf_op jit(solution)/shard_map/psum | solution.py:43
  285.8 10.3 %copy-start.1 = (f32[4,512,512]{2,1,0:T(8,128)S(1)}, f32[4,512,512]{2,1,0:T(8,128)}, u32[]{:S(2)}) copy-start(f32[4,512,512]{2,1,0:T(8,128)} %param.11) | copy-start | bytes 12582916
  309.8 137.7 %copy-start.4 = (f32[2,32,512]{2,1,0:T(8,128)S(1)}, f32[2,32,512]{2,1,0:T(8,128)}, u32[]{:S(2)}) copy-start(f32[2,32,512]{2,1,0:T(8,128)} %param.6) | copy-start | bytes 393220
  332.2 167.8 %all-gather.8.cloned.1.call-start = ((), (), s32[]{:S(2)}) async-start(), calls=%async_computation.7 | async-start | bytes 2228224 | tf_op jit(solution)/shard_map/all_gather | solution.py:32
  449.5 216.0 %all-reduce.8.cloned.1.call-start = ((), (), s32[]{:S(2)}) async-start(), calls=%async_computation.8 | async-start | bytes 4194304 | tf_op jit(solution)/shard_map/psum | solution.py:43
  503.8 10.4 %copy-start.2 = (f32[4,512,512]{2,1,0:T(8,128)S(1)}, f32[4,512,512]{2,1,0:T(8,128)}, u32[]{:S(2)}) copy-start(f32[4,512,512]{2,1,0:T(8,128)} %param.11) | copy-start | bytes 12582916
  528.0 22.3 %copy-start.3 = (f32[2,32,512]{2,0,1:T(2,128)S(1)}, f32[2,32,512]{2,0,1:T(2,128)}, u32[]{:S(2)}) copy-start(f32[2,32,512]{2,0,1:T(2,128)} %fusion.22) | copy-start | bytes 393220
Sparse Core Ops, SparseCore 0:
  11.0 52.8 all-gather.3
  114.3 115.0 all-reduce.3
  232.4 49.5 all-gather.5
  332.3 115.2 all-reduce.5
  450.4 49.5 all-gather.7
  550.4 115.0 all-reduce.7
where the time goes:
time: 680 us; the launch traced here: 675 us
  waiting for transfers between devices  496 us (73%)
  matrix products  81 us (12%)
  blocking collectives  58 us (9%)
  between operations  16.7 us (2%)
  local copies, waits for them, and re-layouts  14 us (2%)
  other arithmetic  8.39 us (1%)
    psum x3, waiting for transfers between devices, hamiltonian(): whole_sums = lax.psum(sector_sums, 'sec')  345 us
    all_gather x3, waiting for transfers between devices, hamiltonian(): gathered = lax.all_gather(iterate, 'op', axis=1, tiled=True)  151 us
    all_to_all x3, blocking collectives, hamiltonian(): lax.all_to_all(split_rows, 'op', split_axis=0, concat_axis=0, tiled=True)  58 us
    dot_general x3, matrix products, hamiltonian(): jnp.einsum('pmk,pnk->mn', left_product, right_ops, precision=highest)  41.5 us
    dot_general x3, matrix products, hamiltonian(): jnp.einsum('pmr,rn->pmn', left_ops, chosen, precision=highest)  30.9 us
  transfers between devices with their start and end apart: 6, of which 6 were waited for; matrix products, arithmetic and copies ran while one was open for 0% of the time, Pallas kernels for 0%

commit v1 on v0

--- a/solution.py
+++ b/solution.py
@@ -40,7 +40,7 @@
             target_hot, flat_rows, precision=highest, preferred_element_type=jnp.float32
         )
         sector_sums = sector_sums.reshape(sectors_all, row_count, order_size)
-        whole_sums = lax.psum(sector_sums, "sec")
+        whole_sums = jnp.sum(lax.all_gather(sector_sums, "sec"), axis=0)
         own_sums = lax.dynamic_slice_in_dim(whole_sums, sec_place * sec_local, sec_local, 0)
         return factor * own_sums * live_mask
 

time: 680 us -> 890 us (1.31)
  waiting for transfers between devices: 496 us -> 670 us
  other arithmetic: 8.39 us -> 44.4 us
    all_gather x0 -> x3, waiting for transfers between devices: none -> 526 us  [hamiltonian(): whole_sums = jnp.sum(lax.all_gather(sector_sums, 'sec'), axis=0)]
    psum x3 -> x0, waiting for transfers between devices: 345 us -> none  [hamiltonian(): whole_sums = lax.psum(sector_sums, 'sec')]
    reduce_sum x0 -> x3, other arithmetic: none -> 38.1 us  [hamiltonian(): whole_sums = jnp.sum(lax.all_gather(sector_sums, 'sec'), axis=0)]
where the time goes in v1:
time: 890 us; the launch traced here: 885 us
  waiting for transfers between devices  670 us (75%)
  matrix products  81.3 us (9%)
  blocking collectives  57.9 us (7%)
  other arithmetic  44.4 us (5%)
  between operations  16.5 us (2%)
  local copies, waits for them, and re-layouts  14.4 us (2%)
    all_gather x3, waiting for transfers between devices, hamiltonian(): whole_sums = jnp.sum(lax.all_gather(sector_sums, 'sec'), axis=0)  526 us
    all_gather x3, waiting for transfers between devices, hamiltonian(): gathered = lax.all_gather(iterate, 'op', axis=1, tiled=True)  145 us
    all_to_all x3, blocking collectives, hamiltonian(): lax.all_to_all(split_rows, 'op', split_axis=0, concat_axis=0, tiled=True)  57.9 us
    dot_general x3, matrix products, hamiltonian(): jnp.einsum('pmk,pnk->mn', left_product, right_ops, precision=highest)  41.5 us
    reduce_sum x3, other arithmetic, hamiltonian(): whole_sums = jnp.sum(lax.all_gather(sector_sums, 'sec'), axis=0)  38.1 us
    dot_general x3, matrix products, hamiltonian(): jnp.einsum('pmr,rn->pmn', left_ops, chosen, precision=highest)  31.1 us
  transfers between devices with their start and end apart: 6, of which 6 were waited for; matrix products, arithmetic and copies ran while one was open for 0% of the time, Pallas kernels for 0%

profile of v1, /device:TPU:1, one launch (start us, length us, event | category | flops | bytes accessed | tf_op | source)
XLA Modules:
  0.0 885.1 jit_solution(8894595678948539102)
XLA Ops:
  7.2 0.0 all-gather.10.cloned.1.call-start
  7.2 0.7 iota_compare_fusion.1
  8.0 0.7 broadcast_compare_fusion
  8.7 1.7 and_select_fusion.3
  10.4 0.0 all-gather.10.cloned.1.call-update
  10.4 0.0 all-gather.16.cloned.1.call-start
  10.5 1.2 dynamic_slice.23
  13.7 50.3 %all-gather.10.cloned.1.call-done = f32[2,512,512]{2,0,1:T(2,128)} async-done(((f32[2,32,512]{2,0,1:T(2,128)}), f32[2,512,512]{2,0,1:T(2,128)}) %all-gather.10.cloned.1.call-update) | async-done | bytes 2097168 | tf_op jit(solution)/shard_map/all_gather | solution.py:32
  63.9 2.5 constant_dynamic-slice_fusion.2
  66.4 1.3 copy.24
  67.8 10.4 %fusion.19 = f32[512,4,512]{2,0,1:T(8,128)S(1)} fusion(f32[4,512,512]{2,1,0:T(8,128)} %param.10, f32[1,512,512]{1,2,0:T(8,128)S(1)} %copy.24), kind=kOutput, calls=%fused_computation.19 | convolution fusion | flops 6442450944 | bytes 9437184 | tf_op jit(solution)/shard_map/pmr,rn->pmn/dot_general | solution.py:34
  78.2 14.1 %fusion.4 = f32[512,512,1]{1,0,2:T(8,128)S(1)} fusion(f32[4,512,512]{2,1,0:T(8,128)S(1)} %copy-done, f32[512,4,512]{2,0,1:T(8,128)S(1)} %fusion.19), kind=kOutput, calls=%fused_computation.4 | convolution fusion | flops 6442450944 | bytes 9437184 | tf_op jit(solution)/shard_map/pmk,pnk->mn/dot_general | solution.py:35
  92.2 19.3 %all_to_all.15 = f32[16,32,512]{2,1,0:T(8,128)S(1)} all-to-all(f32[16,32,512]{2,1,0:T(8,128)S(1)} %bitcast.83), channel_id=1, replica_groups=mesh['sec'=16,'op'=16] {'op'}, dimensions={0} | all-to-all | bytes 2097152 | tf_op jit(solution)/shard_map/all_to_all | solution.py:37
  111.5 2.9 fusion.12
  114.4 0.0 all-gather.16.cloned.1.call-update
  114.4 0.0 all-gather.12.cloned.1.call-start
  114.4 175.4 %all-gather.16.cloned.1.call-done = f32[512,32,512]{2,0,1:T(8,128)} async-done(((f32[32,32,512]{2,0,1:T(8,128)}), f32[512,32,512]{2,0,1:T(8,128)}) %all-gather.16.cloned.1.call-update) | async-done | bytes 33554448 | tf_op jit(solution)/shard_map/all_gather | solution.py:43
  289.9 12.7 %reduce_sum.27 = f32[32,32,512]{2,0,1:T(8,128)S(1)} reduce(f32[16,32,32,512]{3,1,0,2:T(8,128)} %bitcast.80, f32[]{:T(128)} %constant.29.clone.1), dimensions={0}, to_apply=%region_0.1 | reduce | flops 7864320 | bytes 35651588 | tf_op jit(solution)/shard_map/reduce_sum | solution.py:43
  302.6 1.0 and_select_fusion.2
  303.6 0.0 all-gather.12.cloned.1.call-update
  303.6 0.0 all-gather.18.cloned.1.call-start
  303.6 0.3 copy-done.3
  303.9 47.0 %all-gather.12.cloned.1.call-done = f32[2,512,512]{2,0,1:T(2,128)} async-done(((f32[2,32,512]{2,0,1:T(2,128)}), f32[2,512,512]{2,0,1:T(2,128)}) %all-gather.12.cloned.1.call-update) | async-done | bytes 2097168 | tf_op jit(solution)/shard_map/all_gather | solution.py:32
  351.0 2.5 constant_dynamic-slice_fusion.1
  353.5 1.3 copy.27
  354.8 10.3 %fusion.17 = f32[512,4,512]{2,0,1:T(8,128)S(1)} fusion(f32[4,512,512]{2,1,0:T(8,128)} %param.10, f32[1,512,512]{1,2,0:T(8,128)S(1)} %copy.27), kind=kOutput, calls=%fused_computation.17 | convolution fusion | flops 6442450944 | bytes 9437184 | tf_op jit(solution)/shard_map/pmr,rn->pmn/dot_general | solution.py:34
  365.1 13.7 %fusion.2 = f32[512,512,1]{1,0,2:T(8,128)S(1)} fusion(f32[4,512,512]{2,1,0:T(8,128)S(1)} %copy-done.1, f32[512,4,512]{2,0,1:T(8,128)S(1)} %fusion.17), kind=kOutput, calls=%fused_computation.2 | convolution fusion | flops 6442450944 | bytes 9437184 | tf_op jit(solution)/shard_map/pmk,pnk->mn/dot_general | solution.py:35
  378.8 19.3 %all_to_all.16 = f32[16,32,512]{2,1,0:T(8,128)S(1)} all-to-all(f32[16,32,512]{2,1,0:T(8,128)S(1)} %bitcast.84), channel_id=1, replica_groups=mesh['sec'=16,'op'=16] {'op'}, dimensions={0} | all-to-all | bytes 2097152 | tf_op jit(solution)/shard_map/all_to_all | solution.py:37
  398.1 2.9 fusion.9
  401.0 0.0 all-gather.18.cloned.1.call-update
  401.0 0.0 all-gather.14.cloned.1.call-start
  401.1 175.4 %all-gather.18.cloned.1.call-done = f32[512,32,512]{2,0,1:T(8,128)} async-done(((f32[32,32,512]{2,0,1:T(8,128)}), f32[512,32,512]{2,0,1:T(8,128)}) %all-gather.18.cloned.1.call-update) | async-done | bytes 33554448 | tf_op jit(solution)/shard_map/all_gather | solution.py:43
  576.5 12.7 %reduce_sum.28 = f32[32,32,512]{2,0,1:T(8,128)S(1)} reduce(f32[16,32,32,512]{3,1,0,2:T(8,128)} %bitcast.82, f32[]{:T(128)} %constant.29.clone.1), dimensions={0}, to_apply=%region_1.2 | reduce | flops 7864320 | bytes 35651588 | tf_op jit(solution)/shard_map/reduce_sum | solution.py:43
  589.2 0.9 fusion.22
  590.1 0.0 all-gather.14.cloned.1.call-update
  590.1 0.0 all-gather.20.cloned.1.call-start
  590.2 47.3 %all-gather.14.cloned.1.call-done = f32[2,512,512]{2,0,1:T(2,128)} async-done(((f32[2,32,512]{2,0,1:T(2,128)}), f32[2,512,512]{2,0,1:T(2,128)}) %all-gather.14.cloned.1.call-update) | async-done | bytes 2097168 | tf_op jit(solution)/shard_map/all_gather | solution.py:32
  637.5 2.5 constant_dynamic-slice_fusion
  640.0 1.3 copy.30
  641.3 10.5 %fusion.15 = f32[512,4,512]{2,0,1:T(8,128)S(1)} fusion(f32[4,512,512]{2,1,0:T(8,128)} %param.10, f32[1,512,512]{1,2,0:T(8,128)S(1)} %copy.30), kind=kOutput, calls=%fused_computation.15 | convolution fusion | flops 6442450944 | bytes 9437184 | tf_op jit(solution)/shard_map/pmr,rn->pmn/dot_general | solution.py:34
  651.8 13.7 %fusion = f32[512,512,1]{1,0,2:T(8,128)S(1)} fusion(f32[4,512,512]{2,1,0:T(8,128)S(1)} %copy-done.2, f32[512,4,512]{2,0,1:T(8,128)S(1)} %fusion.15), kind=kOutput, calls=%fused_computation | convolution fusion | flops 6442450944 | bytes 9437184 | tf_op jit(solution)/shard_map/pmk,pnk->mn/dot_general | solution.py:35
  665.6 19.4 %all_to_all.17 = f32[16,32,512]{2,1,0:T(8,128)S(1)} all-to-all(f32[16,32,512]{2,1,0:T(8,128)S(1)} %bitcast.85), channel_id=1, replica_groups=mesh['sec'=16,'op'=16] {'op'}, dimensions={0} | all-to-all | bytes 2097152 | tf_op jit(solution)/shard_map/all_to_all | solution.py:37
  685.0 2.9 fusion.6
  687.9 0.7 copy.34
  688.6 174.8 %all-gather.20.cloned.1.call-done = f32[512,32,512]{2,0,1:T(8,128)} async-done(((f32[32,32,512]{2,0,1:T(8,128)}), f32[512,32,512]{2,0,1:T(8,128)}) %all-gather.20.cloned.1.call-update) | async-done | bytes 33554448 | tf_op jit(solution)/shard_map/all_gather | solution.py:43
  863.4 12.7 %reduce_sum.29 = f32[32,32,512]{2,0,1:T(8,128)S(1)} reduce(f32[16,32,32,512]{3,1,0,2:T(8,128)} %bitcast.81, f32[]{:T(128)} %constant.29.clone.1), dimensions={0}, to_apply=%region_2.3 | reduce | flops 7864320 | bytes 35651588 | tf_op jit(solution)/shard_map/reduce_sum | solution.py:43
  876.1 1.3 fusion.24
  877.4 0.7 copy.33
  (15 shorter events, 0.1 us)
Async XLA Ops:
  7.2 56.8 %all-gather.10.cloned.1.call-start = ((), (), s32[]{:S(2)}) async-start(), calls=%async_computation.3 | async-start | bytes 2228224 | tf_op jit(solution)/shard_map/all_gather | solution.py:32
  10.4 279.4 %all-gather.16.cloned.1.call-start = ((), (), s32[]{:S(2)}) async-start(), calls=%async_computation.6 | async-start | bytes 35651584 | tf_op jit(solution)/shard_map/all_gather | solution.py:43
  67.8 10.4 %copy-start = (f32[4,512,512]{2,1,0:T(8,128)S(1)}, f32[4,512,512]{2,1,0:T(8,128)}, u32[]{:S(2)}) copy-start(f32[4,512,512]{2,1,0:T(8,128)} %param.11) | copy-start | bytes 12582916
  78.2 33.3 %copy-start.6 = (s32[16]{0:T(128)S(1)}, s32[16]{0:T(128)}, u32[]{:S(2)}) copy-start(s32[16]{0:T(128)} %param.9) | copy-start | bytes 196
  114.4 236.6 %all-gather.12.cloned.1.call-start = ((), (), s32[]{:S(2)}) async-start(), calls=%async_computation.4 | async-start | bytes 2228224 | tf_op jit(solution)/shard_map/all_gather | solution.py:32
  302.6 1.4 copy-start.3
  303.6 272.9 %all-gather.18.cloned.1.call-start = ((), (), s32[]{:S(2)}) async-start(), calls=%async_computation.7 | async-start | bytes 35651584 | tf_op jit(solution)/shard_map/all_gather | solution.py:43
  354.8 10.3 %copy-start.1 = (f32[4,512,512]{2,1,0:T(8,128)S(1)}, f32[4,512,512]{2,1,0:T(8,128)}, u32[]{:S(2)}) copy-start(f32[4,512,512]{2,1,0:T(8,128)} %param.11) | copy-start | bytes 12582916
  401.0 236.5 %all-gather.14.cloned.1.call-start = ((), (), s32[]{:S(2)}) async-start(), calls=%async_computation.5 | async-start | bytes 2228224 | tf_op jit(solution)/shard_map/all_gather | solution.py:32
  576.5 12.7 %copy-start.5 = (f32[2,32,512]{2,1,0:T(8,128)S(1)}, f32[2,32,512]{2,1,0:T(8,128)}, u32[]{:S(2)}) copy-start(f32[2,32,512]{2,1,0:T(8,128)} %param.6) | copy-start | bytes 393220
  590.1 273.3 %all-gather.20.cloned.1.call-start = ((), (), s32[]{:S(2)}) async-start(), calls=%async_computation.8 | async-start | bytes 35651584 | tf_op jit(solution)/shard_map/all_gather | solution.py:43
  641.3 10.5 %copy-start.2 = (f32[4,512,512]{2,1,0:T(8,128)S(1)}, f32[4,512,512]{2,1,0:T(8,128)}, u32[]{:S(2)}) copy-start(f32[4,512,512]{2,1,0:T(8,128)} %param.11) | copy-start | bytes 12582916
  665.6 22.4 %copy-start.4 = (f32[2,32,512]{2,0,1:T(2,128)S(1)}, f32[2,32,512]{2,0,1:T(2,128)}, u32[]{:S(2)}) copy-start(f32[2,32,512]{2,0,1:T(2,128)} %fusion.22) | copy-start | bytes 393220
Sparse Core Ops, SparseCore 0:
  11.0 52.8 all-gather.9
  114.5 175.3 all-gather.15
  303.7 47.2 all-gather.11
  401.1 175.3 all-gather.17
  590.3 47.2 all-gather.13
  688.0 175.3 all-gather.19
